TPU v7x, 128 devices: a whole 4x4x4 slice. The times are simulated.
128 devices in a mesh: var: 8 (over x, y_lo), space: 16 (over z, y_hi, core).
Axes of the slice: x: 4, y: 4 (y_hi: 2, y_lo: 2; y = y_hi * 2 + y_lo), z: 4, core: 2. Of those that a mesh axis runs over, the one named last changes fastest.
Arguments:
- pixels: bfloat16 [64, 1024, 4096], P('var', 'space'), may hold values from -6 to 6
- counts: int32 [64, 64, 256], P('var', 'space'), may hold values from 0 to 256
- embed_weight: bfloat16 [64, 32, 32, 512], P('var'), may hold values from -0.1875 to 0.1875
- var_embed: bfloat16 [64, 512], P('var'), may hold values from -3 to 3
- query: float32 [512], replicated, may hold values from -140 to 140
- key_weight: bfloat16 [512, 512], replicated, may hold values from -0.25 to 0.25
- value_weight: bfloat16 [512, 512], replicated, may hold values from -0.25 to 0.25
- out_weight: bfloat16 [512, 512], replicated, may hold values from -0.25 to 0.25
Outputs:
- aggregated: bfloat16 [64, 256, 512], P('space', 'var')
All inputs are finite; a program needn't handle non-finite values.
Results may differ from a plain program's by a relative error of at most 0.011.
Values may be sent and summed in bfloat16 or wider, within the bound.
No kernel may reach another device: no remote copies, remote signals or barrier semaphores. Data moves between devices by JAX's collectives and lax.ppermute only.
A program may use at most 128 MiB of HBM per device.

v0:
```python
import functools
import math

import jax
import jax.numpy as jnp
from jax import lax
from jax.experimental import pallas as pl
from jax.experimental.pallas import tpu as pltpu
from jax.sharding import PartitionSpec as P

HEADS = 8
HEAD = 64
PATCH = 16
D = 512
COLS = 4096
PC = 256
LANES = 128
TILES = COLS // LANES
VPD = 8
DEVS = 8
OWN = PC // DEVS
MESSAGE = 2 * OWN + 8
BF = jnp.bfloat16
F32 = jnp.float32
NT = (((1,), (1,)), ((), ()))
SPARE = 8192


def three_parts(x):
    high = x.astype(BF)
    rest = x - high.astype(F32)
    middle = rest.astype(BF)
    return high, middle, (rest - middle.astype(F32)).astype(BF)


def relayout_group(rows, stage, edge_stage, out):
    for t in range(TILES):
        stage[t * 8 : t * 8 + 8, :] = rows[:, t * LANES : (t + 1) * LANES]
    skewed = [
        pltpu.roll(stage[pl.ds(r, TILES, stride=8), :].astype(BF), (16 * r + 8) % LANES, 1) for r in range(8)
    ]
    lane = lax.broadcasted_iota(jnp.int32, (TILES, LANES), 1)
    level = [skewed[(-k) % 8] for k in range(8)]
    for bit in (1, 2, 4):
        chosen = ((lane // 16) & bit) != 0
        level = [jnp.where(chosen, level[(k - bit) % 8], level[k]) for k in range(8)]
    for k in range(1, 8):
        out[k * TILES : (k + 1) * TILES, :] = pltpu.roll(level[k], (-16 * k) % LANES, 1)
    edge_stage[8 : 8 + TILES, :] = level[0].astype(F32)
    left = (lane % 16) < 8
    out[0:TILES, :] = jnp.where(left, edge_stage[7 : 7 + TILES, :].astype(BF), level[0])
    out[8 * TILES : 9 * TILES, :] = jnp.where(left, level[0], edge_stage[9 : 9 + TILES, :].astype(BF))


def permutation():
    row = lax.broadcasted_iota(jnp.int32, (PC, PC), 0)
    col = lax.broadcasted_iota(jnp.int32, (PC, PC), 1)
    same = ((row // 8) == (col % TILES)) & ((row % 8) == (col // TILES))
    return jnp.where(same, 1.0, 0.0).astype(BF)


def embed_kernel(edge, *refs):
    if edge:
        far_ref, near_ref, ext_hbm, *refs = refs
        odd_tile = lax.rem(lax.axis_index("space"), 2) == 1
    else:
        query_hbm, key_hbm, value_hbm, *refs = refs
    px_hbm, w_hbm, cnt_hbm, ve_hbm, msg_ref, *refs = refs
    if not edge:
        ext_out, *refs = refs
    (px, w, ext, cnt_ref, ve_ref, a_even, a_odd, stage_even, stage_odd, edges, tok_even, tok_odd, bias_ref, off_ref,
     top_ref, tot_ref, acc_ref, px_sem, w_sem, sem, *more) = refs
    rows = (0, 3) if edge else (1, 2)
    starts = (0, 4) if edge else (0, 2)

    def px_copy(v):
        return pltpu.make_async_copy(px_hbm.at[v], px.at[v], px_sem.at[v])

    def w_copy(v):
        return pltpu.make_async_copy(w_hbm.at[v], w.at[v], w_sem.at[v])

    small = [(cnt_hbm, cnt_ref), (ve_hbm, ve_ref)]
    if edge:
        small.append((ext_hbm.at[0 : D + 32], ext))
    else:
        query_ref, key_ref, value_ref = more
        small += [(query_hbm, query_ref), (key_hbm, key_ref), (value_hbm, value_ref)]
    small = [pltpu.make_async_copy(src, dst, sem.at[n]) for n, (src, dst) in enumerate(small)]
    for copy in small[:2]:
        copy.start()
    px_copy(0).start()
    for copy in small[2:]:
        copy.start()
    w_copy(0).start()
    px_copy(1).start()

    def relayout(v, a_ref, stage):
        body = px[v].astype(F32)
        if edge:
            far, near = far_ref[v].astype(F32), near_ref[v].astype(F32)
            groups = [jnp.where(odd_tile, near, far), body[0:8], body[8:16], body[16:24],
                      body[40:48], body[48:56], body[56:64], jnp.where(odd_tile, far, near)]
        else:
            groups = [body[8 * n : 8 * n + 8] for n in range(1, 7)]
        for n, group in enumerate(groups):
            relayout_group(group, stage.at[n], edges.at[n], a_ref.at[n])

    def embed_tokens(v, a_ref, tok):
        a = jnp.concatenate(
            [
                jnp.concatenate([a_ref[start + g, b * TILES : b * TILES + PC, :] for g in range(4) for b in range(2)], 1)
                for start in starts
            ],
            0,
        )
        weight = jnp.concatenate(
            [w[v, 8 * g : 8 * g + 8, 16 * b : 16 * b + 16, :].reshape(LANES, D) for g in range(4) for b in range(2)], 0
        )
        tok[...] = (jnp.dot(a, weight, preferred_element_type=F32) + off_ref[v]).astype(BF)

    def attend(v, tok):
        both = lax.dot_general(ext[...], tok[...], NT, preferred_element_type=F32)
        scores = both[0:8] + both[8:16] + both[16:24] + bias_ref[v]
        old = top_ref[...]
        top = jnp.maximum(old, scores)
        decay = jnp.exp(old - top)
        fresh = jnp.exp(scores - top)
        top_ref[...] = top
        tot_ref[...] = tot_ref[...] * decay + fresh
        for h in range(HEADS):
            at = slice(h * HEAD, (h + 1) * HEAD)
            acc_ref[at, :] = acc_ref[at, :] * decay[h : h + 1] + both[32 + h * HEAD : 32 + (h + 1) * HEAD] * fresh[h : h + 1]

    edges[...] = jnp.zeros_like(edges)
    perm = permutation()
    small[0].wait()
    small[1].wait()
    valid = jnp.concatenate([cnt_ref[v].astype(F32) for v in range(VPD)], 0).astype(BF)
    bias = jnp.log((1.0 + jnp.dot(valid, perm, preferred_element_type=F32)) / (1.0 + PATCH * PATCH))
    offsets = ve_ref[...].astype(F32)
    for v in range(VPD):
        off_ref[v] = offsets[v : v + 1]
        bias_ref[v] = jnp.concatenate([bias[4 * v + row : 4 * v + row + 1] for row in rows], 1)
    top_ref[...] = jnp.full_like(top_ref, -1e30)
    tot_ref[...] = jnp.zeros_like(tot_ref)
    acc_ref[...] = jnp.zeros_like(acc_ref)
    px_copy(0).wait()
    w_copy(1).start()
    px_copy(2).start()
    relayout(0, a_even, stage_even)
    w_copy(2).start()
    px_copy(3).start()
    w_copy(0).wait()
    px_copy(1).wait()
    for copy in small[2:]:
        copy.wait()
    if not edge:
        head = lax.broadcasted_iota(jnp.int32, (HEADS, D), 0)
        col = lax.broadcasted_iota(jnp.int32, (HEADS, D), 1)
        spread = jnp.where(col // HEAD == head, jnp.broadcast_to(query_ref[...], (HEADS, D)), 0.0)
        parts = lax.dot_general(jnp.concatenate(three_parts(spread), 0), key_ref[...], NT, preferred_element_type=F32)
        kq = (parts[0:8] + parts[8:16] + parts[16:24]) / math.sqrt(HEAD)
        ext[32 : D + 32, :] = value_ref[...].T
        ext[0:32, :] = jnp.concatenate((*three_parts(kq), jnp.zeros((8, D), BF)), 0)
        ext_copy = pltpu.make_async_copy(ext, ext_out.at[0 : D + 32], sem.at[0])
        ext_copy.start()
    embed_tokens(0, a_even, tok_even)
    relayout(1, a_odd, stage_odd)

    def pair(step, _):
        odd = 2 * step + 1

        @pl.when(step < VPD // 2 - 2)
        def _():
            for v in (odd + 2, odd + 3):
                w_copy(v).start()
                px_copy(v + 1).start()

        @pl.when(step == VPD // 2 - 2)
        def _():
            w_copy(VPD - 1).start()

        for v in (odd, odd + 1):
            w_copy(v).wait()
            px_copy(v + 1).wait()
        embed_tokens(odd, a_odd, tok_odd)
        attend(odd - 1, tok_even)
        relayout(odd + 1, a_even, stage_even)
        embed_tokens(odd + 1, a_even, tok_even)
        attend(odd, tok_odd)
        relayout(odd + 2, a_odd, stage_odd)
        return 0

    lax.fori_loop(0, VPD // 2 - 1, pair, 0)
    w_copy(VPD - 1).wait()
    embed_tokens(VPD - 1, a_odd, tok_odd)
    attend(VPD - 2, tok_even)
    attend(VPD - 1, tok_odd)
    if not edge:
        ext_copy.wait()

    lane = lax.broadcasted_iota(jnp.int32, (24, LANES), 1)
    total = tot_ref[...]
    parts = jnp.concatenate(three_parts(top_ref[...] + jnp.log(total)), 0)
    sums = []
    for n in range(2):
        half = slice(n * PC, (n + 1) * PC)
        weighted = jnp.concatenate(
            [acc_ref[h * HEAD : (h + 1) * HEAD, half] / total[h : h + 1, half] for h in range(HEADS)], 0
        ).astype(BF)
        natural = lax.dot_general(perm, weighted, NT, preferred_element_type=F32).astype(BF)
        for d in range(DEVS):
            msg_ref[d, n * OWN : (n + 1) * OWN, :] = natural[d * OWN : (d + 1) * OWN]
        sums.append(lax.dot_general(parts[:, half], perm, NT, preferred_element_type=F32))
    base = 2 * OWN if edge else 0
    for d in range(DEVS):
        spot = d * OWN // LANES * LANES
        picked = jnp.zeros((24, LANES), F32)
        for n in range(2):
            moved = pltpu.roll(sums[n][:, spot : spot + LANES], (base + n * OWN - d * OWN) % LANES, 1)
            picked = jnp.where(lane // OWN == base // OWN + n, moved, picked)
        wide = jnp.concatenate([picked[0:8], picked[8:16], picked[16:24], jnp.zeros((8, LANES), F32)], 1)
        msg_ref[d, 2 * OWN : MESSAGE, :] = wide.astype(BF)


def embed(edge, extras, pixels, weight, counts, var_embed):
    groups = 8 if edge else 6
    hbm = pl.BlockSpec(memory_space=pltpu.HBM)
    vmem = pl.BlockSpec(memory_space=pltpu.VMEM)
    out_shape = [jax.ShapeDtypeStruct((DEVS, MESSAGE, D), BF)]
    scratch = [
        pltpu.VMEM((VPD, 64, COLS), BF),
        pltpu.VMEM((VPD, 32, 32, D), BF),
        pltpu.VMEM((D + 32, D), BF),
        pltpu.VMEM((VPD, 4, PC), jnp.int32),
        pltpu.VMEM((VPD, D), BF),
        pltpu.VMEM((groups, PC + TILES, LANES), BF),
        pltpu.VMEM((groups, PC + TILES, LANES), BF),
        pltpu.VMEM((groups, TILES * 8, LANES), F32),
        pltpu.VMEM((groups, TILES * 8, LANES), F32),
        pltpu.VMEM((groups, TILES + 16, LANES), F32),
        pltpu.VMEM((D, D), BF),
        pltpu.VMEM((D, D), BF),
        pltpu.VMEM((VPD, 1, 2 * PC), F32),
        pltpu.VMEM((VPD, 1, D), F32),
        pltpu.VMEM((HEADS, 2 * PC), F32),
        pltpu.VMEM((HEADS, 2 * PC), F32),
        pltpu.VMEM((D, 2 * PC), F32),
        pltpu.SemaphoreType.DMA((VPD,)),
        pltpu.SemaphoreType.DMA((VPD,)),
        pltpu.SemaphoreType.DMA((5,)),
    ]
    if not edge:
        out_shape.append(jax.ShapeDtypeStruct((SPARE, D), BF))
        scratch += [pltpu.VMEM((1, D), F32), pltpu.VMEM((D, D), BF), pltpu.VMEM((D, D), BF)]
    return pl.pallas_call(
        functools.partial(embed_kernel, edge),
        in_specs=[vmem if edge else hbm] * 2 + [hbm] * 5,
        out_specs=[vmem, hbm][: len(out_shape)],
        out_shape=out_shape,
        scratch_shapes=scratch,
        compiler_params=pltpu.CompilerParams(vmem_limit_bytes=(52 if edge else 56) * 2**20),
        cost_estimate=pl.CostEstimate(flops=8 * 2 * 512 * (1024 + 512) * 512, bytes_accessed=13 * 2**20, transcendentals=0),
        name="embed_edge" if edge else "embed_inner",
    )(*extras, pixels, weight, counts, var_embed)


def finish_kernel(inner_ref, outer_ref, wo_ref, out_ref):
    lane = lax.broadcasted_iota(jnp.int32, (HEADS, LANES), 1)
    sums = []
    for s in range(DEVS):
        a = inner_ref[s, 2 * OWN : MESSAGE, :].astype(F32)
        b = outer_ref[s, 2 * OWN : MESSAGE, :].astype(F32)
        a = a[:, 0:LANES] + a[:, LANES : 2 * LANES] + a[:, 2 * LANES : 3 * LANES]
        b = b[:, 0:LANES] + b[:, LANES : 2 * LANES] + b[:, 2 * LANES : 3 * LANES]
        sums.append(jnp.where(lane < 2 * OWN, a, b))
    top = functools.reduce(jnp.maximum, sums)
    parts = [jnp.exp(x - top) for x in sums]
    scale = 1.0 / functools.reduce(jnp.add, parts)
    shares = []
    for part in parts:
        share = part * scale
        high = share.astype(BF).astype(F32)
        shares += [high, share - high]
    shares = jnp.concatenate(shares, 0).T.astype(BF)
    row = lax.broadcasted_iota(jnp.int32, (LANES, D), 0)
    col = lax.broadcasted_iota(jnp.int32, (LANES, D), 1)
    spread = jnp.where((row < 16) & (col // HEAD == row % HEADS), 1.0, 0.0).astype(BF)
    turned = [pltpu.roll(shares, (-16 * s) % LANES, 1) if s else shares for s in range(DEVS)]
    wide = jnp.dot(jnp.concatenate(turned, 0), spread, preferred_element_type=F32)
    mixture = jnp.zeros((LANES, D), F32)
    for s in range(DEVS):
        values = jnp.concatenate([inner_ref[s, 0 : 2 * OWN, :], outer_ref[s, 0 : 2 * OWN, :]], 0)
        mixture = mixture + wide[s * LANES : (s + 1) * LANES] * values.astype(F32)
    result = jnp.dot(mixture.astype(BF), wo_ref[...], preferred_element_type=F32).astype(BF)
    for n, row in enumerate((1, 2, 0, 3)):
        out_ref[row] = result[n * OWN : (n + 1) * OWN]


def finish(inner, outer, out_weight):
    return pl.pallas_call(
        finish_kernel,
        out_shape=jax.ShapeDtypeStruct((4, OWN, D), BF),
        compiler_params=pltpu.CompilerParams(vmem_limit_bytes=24 * 2**20),
        cost_estimate=pl.CostEstimate(flops=2 * 128 * 512 * 512, bytes_accessed=2**21, transcendentals=0),
        name="finish",
    )(inner, outer, out_weight)


def exchange(msg):
    return lax.all_to_all(msg, "var", 0, 0)


def shards(pixels, counts, embed_weight, var_embed, query, key_weight, value_weight, out_weight):
    count = lax.axis_size("space")
    odd = lax.rem(lax.axis_index("space"), 2)
    far_pairs = [(i, i + 1) for i in range(1, count - 1, 2)]
    near_pairs = [(i, i + 1) for i in range(0, count - 1, 2)]
    both_ways = lambda pairs: pairs + [(b, a) for a, b in pairs]
    reach = PATCH // 2
    last = pixels.shape[1] - reach
    far = lax.ppermute(lax.dynamic_slice_in_dim(pixels, odd * last, reach, 1), "space", both_ways(far_pairs))
    near = lax.ppermute(lax.dynamic_slice_in_dim(pixels, (1 - odd) * last, reach, 1), "space", both_ways(near_pairs))
    rest = (pixels, embed_weight, counts, var_embed)
    inner, ext = embed(False, (query.reshape(1, D), key_weight, value_weight), *rest)
    inner = exchange(inner)
    (outer,) = embed(True, (far, near, ext), *rest)
    outer = exchange(outer)
    return finish(inner, outer, out_weight)


def solution(mesh):
    return jax.shard_map(
        shards,
        mesh=mesh,
        in_specs=(
            P("var", "space", None),
            P("var", "space", None),
            P("var", None, None, None),
            P("var", None),
            P(),
            P(),
            P(),
            P(),
        ),
        out_specs=P("space", "var", None),
        check_vma=False,
    )
```

profile of v0, /device:TPU:96, one launch (start us, length us, event | category | flops | bytes accessed | tf_op | source)
XLA Modules:
  0.0 51.0 jit_solution(3018216260432806744)
XLA Ops:
  0.0 1.3 %constant_dynamic-slice_fusion = (bf16[8,8,4096]{2,1,0:T(8,128)(2,1)S(1)}, bf16[8,8,4096]{2,1,0:T(8,128)(2,1)S(1)}) fusion(bf16[8,64,4096]{2,1,0:T(8,128)(2,1)} %refs_3_.3, s32[]{:T(128)S(6)} %select_n.7, s32[]{:T(128)S(6)} %select_n.6), kind=kLoop, calls=%fused_computation | loop fusion | bytes 2097160 | tf_op jit(solution)/shard_map/dynamic_slice | solution.py:323
  1.3 4.4 %collective-permute-start = (bf16[8,8,4096]{2,1,0:T(8,128)(2,1)S(1)}, bf16[8,8,4096]{2,1,0:T(8,128)(2,1)S(1)}, u32[]{:S(2)}, u32[]{:S(2)}) collective-permute-start(bf16[8,8,4096]{2,1,0:T(8,128)(2,1)S(1)} %get-tuple-element.10), channel_id=1, source_target_pairs={{1,2},{3,4},{5,6},{7,8},{9,10},{11,12},{13,14},{2,1},{4,3},{6,5},{... | collective-permute-start | bytes 1572872 | tf_op jit(solution)/shard_map/ppermute | solution.py:322
  5.7 0.9 %collective-permute-start.1 = (bf16[8,8,4096]{2,1,0:T(8,128)(2,1)S(1)}, bf16[8,8,4096]{2,1,0:T(8,128)(2,1)S(1)}, u32[]{:S(2)}, u32[]{:S(2)}) collective-permute-start(bf16[8,8,4096]{2,1,0:T(8,128)(2,1)S(1)} %get-tuple-element.9), channel_id=1, source_target_pairs={{0,1},{2,3},{4,5},{6,7},{8,9},{10,11},{12,13},{14,15},{1,0},{3,2},... | collective-permute-start | bytes 1572872 | tf_op jit(solution)/shard_map/ppermute | solution.py:323
  6.6 0.0 copy-start.1
  6.6 0.0 copy-start.2
  6.6 11.6 %embed_inner.1 = (bf16[8,72,512]{2,1,0:T(8,128)(2,1)}, bf16[8192,512]{1,0:T(8,128)(2,1)}) custom-call(f32[1,512]{1,0:T(1,128)} %bitcast.1, bf16[512,512]{1,0:T(8,128)(2,1)} %refs_1_.1, bf16[512,512]{1,0:T(8,128)(2,1)} %refs_2_.1, bf16[8,64,4096]{2,1,0:T(8,128)(2,1)} %refs_3_.3, bf16[8,32,32,512]{3,2,1,0:T(8,128)(2,1)} %refs_4_.3, s32[8,4,256]{2,1,0:T(4,128)} %refs_5_.3, ...), custom_call_target="tpu_custom_call" | custom-call | flops 6442450944 | bytes 13631488 | tf_op jit(solution)/shard_map/embed_inner/pallas_call | solution.py:256
  18.1 4.4 %all-to-all-start = ((bf16[8,72,512]{2,1,0:T(8,128)(2,1)}), bf16[8,72,512]{2,1,0:T(8,128)(2,1)S(1)}, u32[]{:S(2)}, u32[]{:S(2)}) async-start(bf16[8,72,512]{2,1,0:T(8,128)(2,1)} %get-tuple-element.7), calls=%async_computation | async-start | bytes 1179648 | tf_op jit(solution)/shard_map/all_to_all | solution.py:311
  22.6 0.0 collective-permute-done.refs_0_
  22.6 0.0 collective-permute-done.1.refs_1_
  22.6 0.0 copy-done.1
  22.6 0.0 copy-done.2
  22.6 0.0 copy-start
  22.6 11.0 %embed_edge.1 = bf16[8,72,512]{2,1,0:T(8,128)(2,1)S(1)} custom-call(bf16[8,8,4096]{2,1,0:T(8,128)(2,1)S(1)} %collective-permute-done.refs_0_, bf16[8,8,4096]{2,1,0:T(8,128)(2,1)S(1)} %collective-permute-done.1.refs_1_, bf16[8192,512]{1,0:T(8,128)(2,1)} %get-tuple-element.8.refs_2_, bf16[8,64,4096]{2,1,0:T(8,128)(2,1)} %refs_3_.3, ...), custom_call_target="tpu_custom_call" | custom-call | flops 6442450944 | bytes 13631488 | tf_op jit(solution)/shard_map/embed_edge/pallas_call | solution.py:256
  33.7 0.0 all-to-all-done.inner_ref
  33.7 16.0 %all_to_all.10.outer_ref = bf16[8,72,512]{2,1,0:T(8,128)(2,1)S(1)} all-to-all(bf16[8,72,512]{2,1,0:T(8,128)(2,1)S(1)} %embed_edge.1), channel_id=1, replica_groups=mesh['var'=8,'space'=16] {'var'}, dimensions={0} | all-to-all | bytes 1179648 | tf_op jit(solution)/shard_map/all_to_all | solution.py:311
  49.6 0.0 copy-done
  49.6 1.4 %finish.1 = bf16[4,32,512]{2,1,0:T(8,128)(2,1)} custom-call(bf16[8,72,512]{2,1,0:T(8,128)(2,1)S(1)} %all-to-all-done.inner_ref, bf16[8,72,512]{2,1,0:T(8,128)(2,1)S(1)} %all_to_all.10.outer_ref, bf16[512,512]{1,0:T(8,128)(2,1)S(1)} %copy-done), custom_call_target="tpu_custom_call" | custom-call | flops 67108864 | bytes 2097152 | tf_op jit(solution)/shard_map/finish/pallas_call | solution.py:301
Async XLA Ops:
  1.3 21.3 %collective-permute-start = (bf16[8,8,4096]{2,1,0:T(8,128)(2,1)S(1)}, bf16[8,8,4096]{2,1,0:T(8,128)(2,1)S(1)}, u32[]{:S(2)}, u32[]{:S(2)}) collective-permute-start(bf16[8,8,4096]{2,1,0:T(8,128)(2,1)S(1)} %get-tuple-element.10), channel_id=1, source_target_pairs={{1,2},{3,4},{5,6},{7,8},{9,10},{11,12},{13,14},{2,1},{4,3},{6,5},{... | collective-permute-start | bytes 1572872 | tf_op jit(solution)/shard_map/ppermute | solution.py:322
  5.7 16.9 %collective-permute-start.1 = (bf16[8,8,4096]{2,1,0:T(8,128)(2,1)S(1)}, bf16[8,8,4096]{2,1,0:T(8,128)(2,1)S(1)}, u32[]{:S(2)}, u32[]{:S(2)}) collective-permute-start(bf16[8,8,4096]{2,1,0:T(8,128)(2,1)S(1)} %get-tuple-element.9), channel_id=1, source_target_pairs={{0,1},{2,3},{4,5},{6,7},{8,9},{10,11},{12,13},{14,15},{1,0},{3,2},... | collective-permute-start | bytes 1572872 | tf_op jit(solution)/shard_map/ppermute | solution.py:323
  6.6 16.0 %copy-start.1 = (s32[8,4,256]{2,1,0:T(4,128)S(1)}, s32[8,4,256]{2,1,0:T(4,128)}, u32[]{:S(2)}) copy-start(s32[8,4,256]{2,1,0:T(4,128)} %refs_5_.3) | copy-start | bytes 98308
  6.6 16.0 %copy-start.2 = (bf16[8,512]{1,0:T(8,128)(2,1)S(1)}, bf16[8,512]{1,0:T(8,128)(2,1)}, u32[]{:S(2)}) copy-start(bf16[8,512]{1,0:T(8,128)(2,1)} %refs_6_.3) | copy-start | bytes 24580
  18.1 15.5 %all-to-all-start = ((bf16[8,72,512]{2,1,0:T(8,128)(2,1)}), bf16[8,72,512]{2,1,0:T(8,128)(2,1)S(1)}, u32[]{:S(2)}, u32[]{:S(2)}) async-start(bf16[8,72,512]{2,1,0:T(8,128)(2,1)} %get-tuple-element.7), calls=%async_computation | async-start | bytes 1179648 | tf_op jit(solution)/shard_map/all_to_all | solution.py:311
  22.6 27.0 %copy-start = (bf16[512,512]{1,0:T(8,128)(2,1)S(1)}, bf16[512,512]{1,0:T(8,128)(2,1)}, u32[]{:S(2)}) copy-start(bf16[512,512]{1,0:T(8,128)(2,1)} %wo_ref.1) | copy-start | bytes 1572868
where the time goes:
time: 51.4 us; the launch traced here: 51 us
  Pallas kernels  24 us (47%)
  blocking collectives  16 us (31%)
  starting transfers between devices  9.73 us (19%)
  local copies, waits for them, and re-layouts  1.28 us (2%)
    pallas_call x2, Pallas kernels, embed(): pl.pallas_call(functools.partial(embed_kernel, edge), in_specs=[vmem if e...  22.6 us
    all_to_all x1, blocking collectives, exchange(): return lax.all_to_all(msg, 'var', 0, 0)  16 us
    all_to_all x1, starting transfers between devices, exchange(): return lax.all_to_all(msg, 'var', 0, 0)  4.43 us
    ppermute x1, starting transfers between devices, shards(): lax.ppermute(lax.dynamic_slice_in_dim(pixels, odd * last, reach, 1), 'spa...  4.38 us
    pallas_call x1, Pallas kernels, finish(): pl.pallas_call(finish_kernel, out_shape=jax.ShapeDtypeStruct((4, OWN, D),...  1.4 us
    dynamic_slice x1, local copies, waits for them, and re-layouts, shards(): lax.dynamic_slice_in_dim(pixels, (1 - odd) * last, reach, 1)  1.27 us
  transfers between devices with their start and end apart: 3, of which 0 were waited for; matrix products, arithmetic and copies ran while one was open for 0% of the time, Pallas kernels for 44%

commit v1 on v0

--- a/solution.py
+++ b/solution.py
@@ -86,10 +86,8 @@
         query_ref, key_ref, value_ref = more
         small += [(query_hbm, query_ref), (key_hbm, key_ref), (value_hbm, value_ref)]
     small = [pltpu.make_async_copy(src, dst, sem.at[n]) for n, (src, dst) in enumerate(small)]
-    for copy in small[:2]:
-        copy.start()
     px_copy(0).start()
-    for copy in small[2:]:
+    for copy in small:
         copy.start()
     w_copy(0).start()
     px_copy(1).start()
@@ -133,14 +131,6 @@
 
     edges[...] = jnp.zeros_like(edges)
     perm = permutation()
-    small[0].wait()
-    small[1].wait()
-    valid = jnp.concatenate([cnt_ref[v].astype(F32) for v in range(VPD)], 0).astype(BF)
-    bias = jnp.log((1.0 + jnp.dot(valid, perm, preferred_element_type=F32)) / (1.0 + PATCH * PATCH))
-    offsets = ve_ref[...].astype(F32)
-    for v in range(VPD):
-        off_ref[v] = offsets[v : v + 1]
-        bias_ref[v] = jnp.concatenate([bias[4 * v + row : 4 * v + row + 1] for row in rows], 1)
     top_ref[...] = jnp.full_like(top_ref, -1e30)
     tot_ref[...] = jnp.zeros_like(tot_ref)
     acc_ref[...] = jnp.zeros_like(acc_ref)
@@ -150,6 +140,14 @@
     relayout(0, a_even, stage_even)
     w_copy(2).start()
     px_copy(3).start()
+    small[0].wait()
+    small[1].wait()
+    valid = jnp.concatenate([cnt_ref[v].astype(F32) for v in range(VPD)], 0).astype(BF)
+    bias = jnp.log((1.0 + jnp.dot(valid, perm, preferred_element_type=F32)) / (1.0 + PATCH * PATCH))
+    offsets = ve_ref[...].astype(F32)
+    for v in range(VPD):
+        off_ref[v] = offsets[v : v + 1]
+        bias_ref[v] = jnp.concatenate([bias[4 * v + row : 4 * v + row + 1] for row in rows], 1)
     w_copy(0).wait()
     px_copy(1).wait()
     for copy in small[2:]:

time: 51.4 us -> 51.3 us (level)
  no operation moved by 1% of the time
where the time goes in v1:
time: 51.3 us; the launch traced here: 50.9 us
  Pallas kernels  23.9 us (47%)
  blocking collectives  15.9 us (31%)
  starting transfers between devices  9.72 us (19%)
  local copies, waits for them, and re-layouts  1.28 us (2%)
    pallas_call x2, Pallas kernels, embed(): pl.pallas_call(functools.partial(embed_kernel, edge), in_specs=[vmem if e...  22.5 us
    all_to_all x1, blocking collectives, exchange(): return lax.all_to_all(msg, 'var', 0, 0)  15.9 us
    all_to_all x1, starting transfers between devices, exchange(): return lax.all_to_all(msg, 'var', 0, 0)  4.42 us
    ppermute x1, starting transfers between devices, shards(): lax.ppermute(lax.dynamic_slice_in_dim(pixels, odd * last, reach, 1), 'spa...  4.38 us
    pallas_call x1, Pallas kernels, finish(): pl.pallas_call(finish_kernel, out_shape=jax.ShapeDtypeStruct((4, OWN, D),...  1.4 us
    dynamic_slice x1, local copies, waits for them, and re-layouts, shards(): lax.dynamic_slice_in_dim(pixels, (1 - odd) * last, reach, 1)  1.27 us
  transfers between devices with their start and end apart: 3, of which 0 were waited for; matrix products, arithmetic and copies ran while one was open for 0% of the time, Pallas kernels for 44%

profile of v1, /device:TPU:96, one launch (start us, length us, event | category | flops | bytes accessed | tf_op | source)
XLA Modules:
  0.0 50.9 jit_solution(6377624240915926987)
XLA Ops:
  0.0 1.3 %constant_dynamic-slice_fusion = (bf16[8,8,4096]{2,1,0:T(8,128)(2,1)S(1)}, bf16[8,8,4096]{2,1,0:T(8,128)(2,1)S(1)}) fusion(bf16[8,64,4096]{2,1,0:T(8,128)(2,1)} %refs_3_.3, s32[]{:T(128)S(6)} %select_n.7, s32[]{:T(128)S(6)} %select_n.6), kind=kLoop, calls=%fused_computation | loop fusion | bytes 2097160 | tf_op jit(solution)/shard_map/dynamic_slice | solution.py:321
  1.3 4.4 %collective-permute-start = (bf16[8,8,4096]{2,1,0:T(8,128)(2,1)S(1)}, bf16[8,8,4096]{2,1,0:T(8,128)(2,1)S(1)}, u32[]{:S(2)}, u32[]{:S(2)}) collective-permute-start(bf16[8,8,4096]{2,1,0:T(8,128)(2,1)S(1)} %get-tuple-element.10), channel_id=1, source_target_pairs={{1,2},{3,4},{5,6},{7,8},{9,10},{11,12},{13,14},{2,1},{4,3},{6,5},{... | collective-permute-start | bytes 1572872 | tf_op jit(solution)/shard_map/ppermute | solution.py:320
  5.7 0.9 %collective-permute-start.1 = (bf16[8,8,4096]{2,1,0:T(8,128)(2,1)S(1)}, bf16[8,8,4096]{2,1,0:T(8,128)(2,1)S(1)}, u32[]{:S(2)}, u32[]{:S(2)}) collective-permute-start(bf16[8,8,4096]{2,1,0:T(8,128)(2,1)S(1)} %get-tuple-element.9), channel_id=1, source_target_pairs={{0,1},{2,3},{4,5},{6,7},{8,9},{10,11},{12,13},{14,15},{1,0},{3,2},... | collective-permute-start | bytes 1572872 | tf_op jit(solution)/shard_map/ppermute | solution.py:321
  6.6 0.0 copy-start.1
  6.6 0.0 copy-start.2
  6.6 11.6 %embed_inner.1 = (bf16[8,72,512]{2,1,0:T(8,128)(2,1)}, bf16[8192,512]{1,0:T(8,128)(2,1)}) custom-call(f32[1,512]{1,0:T(1,128)} %bitcast.1, bf16[512,512]{1,0:T(8,128)(2,1)} %refs_1_.1, bf16[512,512]{1,0:T(8,128)(2,1)} %refs_2_.1, bf16[8,64,4096]{2,1,0:T(8,128)(2,1)} %refs_3_.3, bf16[8,32,32,512]{3,2,1,0:T(8,128)(2,1)} %refs_4_.3, s32[8,4,256]{2,1,0:T(4,128)} %refs_5_.3, ...), custom_call_target="tpu_custom_call" | custom-call | flops 6442450944 | bytes 13631488 | tf_op jit(solution)/shard_map/embed_inner/pallas_call | solution.py:254
  18.2 4.4 %all-to-all-start = ((bf16[8,72,512]{2,1,0:T(8,128)(2,1)}), bf16[8,72,512]{2,1,0:T(8,128)(2,1)S(1)}, u32[]{:S(2)}, u32[]{:S(2)}) async-start(bf16[8,72,512]{2,1,0:T(8,128)(2,1)} %get-tuple-element.7), calls=%async_computation | async-start | bytes 1179648 | tf_op jit(solution)/shard_map/all_to_all | solution.py:309
  22.6 0.0 collective-permute-done.refs_0_
  22.6 0.0 collective-permute-done.1.refs_1_
  22.6 0.0 copy-done.1
  22.6 0.0 copy-done.2
  22.6 0.0 copy-start
  22.6 10.9 %embed_edge.1 = bf16[8,72,512]{2,1,0:T(8,128)(2,1)S(1)} custom-call(bf16[8,8,4096]{2,1,0:T(8,128)(2,1)S(1)} %collective-permute-done.refs_0_, bf16[8,8,4096]{2,1,0:T(8,128)(2,1)S(1)} %collective-permute-done.1.refs_1_, bf16[8192,512]{1,0:T(8,128)(2,1)} %get-tuple-element.8.refs_2_, bf16[8,64,4096]{2,1,0:T(8,128)(2,1)} %refs_3_.3, ...), custom_call_target="tpu_custom_call" | custom-call | flops 6442450944 | bytes 13631488 | tf_op jit(solution)/shard_map/embed_edge/pallas_call | solution.py:254
  33.6 0.0 all-to-all-done.inner_ref
  33.6 15.9 %all_to_all.10.outer_ref = bf16[8,72,512]{2,1,0:T(8,128)(2,1)S(1)} all-to-all(bf16[8,72,512]{2,1,0:T(8,128)(2,1)S(1)} %embed_edge.1), channel_id=1, replica_groups=mesh['var'=8,'space'=16] {'var'}, dimensions={0} | all-to-all | bytes 1179648 | tf_op jit(solution)/shard_map/all_to_all | solution.py:309
  49.5 0.0 copy-done
  49.5 1.4 %finish.1 = bf16[4,32,512]{2,1,0:T(8,128)(2,1)} custom-call(bf16[8,72,512]{2,1,0:T(8,128)(2,1)S(1)} %all-to-all-done.inner_ref, bf16[8,72,512]{2,1,0:T(8,128)(2,1)S(1)} %all_to_all.10.outer_ref, bf16[512,512]{1,0:T(8,128)(2,1)S(1)} %copy-done), custom_call_target="tpu_custom_call" | custom-call | flops 67108864 | bytes 2097152 | tf_op jit(solution)/shard_map/finish/pallas_call | solution.py:299
Async XLA Ops:
  1.3 21.3 %collective-permute-start = (bf16[8,8,4096]{2,1,0:T(8,128)(2,1)S(1)}, bf16[8,8,4096]{2,1,0:T(8,128)(2,1)S(1)}, u32[]{:S(2)}, u32[]{:S(2)}) collective-permute-start(bf16[8,8,4096]{2,1,0:T(8,128)(2,1)S(1)} %get-tuple-element.10), channel_id=1, source_target_pairs={{1,2},{3,4},{5,6},{7,8},{9,10},{11,12},{13,14},{2,1},{4,3},{6,5},{... | collective-permute-start | bytes 1572872 | tf_op jit(solution)/shard_map/ppermute | solution.py:320
  5.7 16.9 %collective-permute-start.1 = (bf16[8,8,4096]{2,1,0:T(8,128)(2,1)S(1)}, bf16[8,8,4096]{2,1,0:T(8,128)(2,1)S(1)}, u32[]{:S(2)}, u32[]{:S(2)}) collective-permute-start(bf16[8,8,4096]{2,1,0:T(8,128)(2,1)S(1)} %get-tuple-element.9), channel_id=1, source_target_pairs={{0,1},{2,3},{4,5},{6,7},{8,9},{10,11},{12,13},{14,15},{1,0},{3,2},... | collective-permute-start | bytes 1572872 | tf_op jit(solution)/shard_map/ppermute | solution.py:321
  6.6 16.0 %copy-start.1 = (s32[8,4,256]{2,1,0:T(4,128)S(1)}, s32[8,4,256]{2,1,0:T(4,128)}, u32[]{:S(2)}) copy-start(s32[8,4,256]{2,1,0:T(4,128)} %refs_5_.3) | copy-start | bytes 98308
  6.6 16.0 %copy-start.2 = (bf16[8,512]{1,0:T(8,128)(2,1)S(1)}, bf16[8,512]{1,0:T(8,128)(2,1)}, u32[]{:S(2)}) copy-start(bf16[8,512]{1,0:T(8,128)(2,1)} %refs_6_.3) | copy-start | bytes 24580
  18.2 15.4 %all-to-all-start = ((bf16[8,72,512]{2,1,0:T(8,128)(2,1)}), bf16[8,72,512]{2,1,0:T(8,128)(2,1)S(1)}, u32[]{:S(2)}, u32[]{:S(2)}) async-start(bf16[8,72,512]{2,1,0:T(8,128)(2,1)} %get-tuple-element.7), calls=%async_computation | async-start | bytes 1179648 | tf_op jit(solution)/shard_map/all_to_all | solution.py:309
  22.6 26.9 %copy-start = (bf16[512,512]{1,0:T(8,128)(2,1)S(1)}, bf16[512,512]{1,0:T(8,128)(2,1)}, u32[]{:S(2)}) copy-start(bf16[512,512]{1,0:T(8,128)(2,1)} %wo_ref.1) | copy-start | bytes 1572868

commit v2 on v1

--- a/solution.py
+++ b/solution.py
@@ -67,6 +67,7 @@
         query_hbm, key_hbm, value_hbm, *refs = refs
     px_hbm, w_hbm, cnt_hbm, ve_hbm, msg_ref, *refs = refs
     if not edge:
+        msg_hbm = msg_ref
         ext_out, *refs = refs
     (px, w, ext, cnt_ref, ve_ref, a_even, a_odd, stage_even, stage_odd, edges, tok_even, tok_odd, bias_ref, off_ref,
      top_ref, tot_ref, acc_ref, px_sem, w_sem, sem, *more) = refs
@@ -83,7 +84,7 @@
     if edge:
         small.append((ext_hbm.at[0 : D + 32], ext))
     else:
-        query_ref, key_ref, value_ref = more
+        query_ref, key_ref, value_ref, msg_ref, msg_sem = more
         small += [(query_hbm, query_ref), (key_hbm, key_ref), (value_hbm, value_ref)]
     small = [pltpu.make_async_copy(src, dst, sem.at[n]) for n, (src, dst) in enumerate(small)]
     px_copy(0).start()
@@ -200,7 +201,7 @@
     lane = lax.broadcasted_iota(jnp.int32, (24, LANES), 1)
     total = tot_ref[...]
     parts = jnp.concatenate(three_parts(top_ref[...] + jnp.log(total)), 0)
-    sums = []
+    sums, row_copies = [], []
     for n in range(2):
         half = slice(n * PC, (n + 1) * PC)
         weighted = jnp.concatenate(
@@ -209,6 +210,10 @@
         natural = lax.dot_general(perm, weighted, NT, preferred_element_type=F32).astype(BF)
         for d in range(DEVS):
             msg_ref[d, n * OWN : (n + 1) * OWN, :] = natural[d * OWN : (d + 1) * OWN]
+        if not edge:
+            at = pl.ds(n * OWN, OWN)
+            row_copies.append(pltpu.make_async_copy(msg_ref.at[:, at], msg_hbm.at[:, at], msg_sem.at[n]))
+            row_copies[-1].start()
         sums.append(lax.dot_general(parts[:, half], perm, NT, preferred_element_type=F32))
     base = 2 * OWN if edge else 0
     for d in range(DEVS):
@@ -219,6 +224,12 @@
             picked = jnp.where(lane // OWN == base // OWN + n, moved, picked)
         wide = jnp.concatenate([picked[0:8], picked[8:16], picked[16:24], jnp.zeros((8, LANES), F32)], 1)
         msg_ref[d, 2 * OWN : MESSAGE, :] = wide.astype(BF)
+    if not edge:
+        at = pl.ds(2 * OWN, MESSAGE - 2 * OWN)
+        row_copies.append(pltpu.make_async_copy(msg_ref.at[:, at], msg_hbm.at[:, at], msg_sem.at[2]))
+        row_copies[-1].start()
+        for copy in row_copies:
+            copy.wait()
 
 
 def embed(edge, extras, pixels, weight, counts, var_embed):
@@ -250,11 +261,17 @@
     ]
     if not edge:
         out_shape.append(jax.ShapeDtypeStruct((SPARE, D), BF))
-        scratch += [pltpu.VMEM((1, D), F32), pltpu.VMEM((D, D), BF), pltpu.VMEM((D, D), BF)]
+        scratch += [
+            pltpu.VMEM((1, D), F32),
+            pltpu.VMEM((D, D), BF),
+            pltpu.VMEM((D, D), BF),
+            pltpu.VMEM((DEVS, MESSAGE, D), BF),
+            pltpu.SemaphoreType.DMA((3,)),
+        ]
     return pl.pallas_call(
         functools.partial(embed_kernel, edge),
         in_specs=[vmem if edge else hbm] * 2 + [hbm] * 5,
-        out_specs=[vmem, hbm][: len(out_shape)],
+        out_specs=[vmem] if edge else [hbm, hbm],
         out_shape=out_shape,
         scratch_shapes=scratch,
         compiler_params=pltpu.CompilerParams(vmem_limit_bytes=(52 if edge else 56) * 2**20),

time: 51.3 us -> 51.2 us (level)
  no operation moved by 1% of the time
where the time goes in v2:
time: 51.2 us; the launch traced here: 50.9 us
  Pallas kernels  23.8 us (46%)
  blocking collectives  15.9 us (31%)
  starting transfers between devices  9.72 us (19%)
  local copies, waits for them, and re-layouts  1.28 us (2%)
    pallas_call x2, Pallas kernels, embed(): pl.pallas_call(functools.partial(embed_kernel, edge), in_specs=[vmem if e...  22.4 us
    all_to_all x1, blocking collectives, exchange(): return lax.all_to_all(msg, 'var', 0, 0)  15.9 us
    all_to_all x1, starting transfers between devices, exchange(): return lax.all_to_all(msg, 'var', 0, 0)  4.42 us
    ppermute x1, starting transfers between devices, shards(): lax.ppermute(lax.dynamic_slice_in_dim(pixels, odd * last, reach, 1), 'spa...  4.38 us
    pallas_call x1, Pallas kernels, finish(): pl.pallas_call(finish_kernel, out_shape=jax.ShapeDtypeStruct((4, OWN, D),...  1.4 us
    dynamic_slice x1, local copies, waits for them, and re-layouts, shards(): lax.dynamic_slice_in_dim(pixels, (1 - odd) * last, reach, 1)  1.27 us
  transfers between devices with their start and end apart: 3, of which 0 were waited for; matrix products, arithmetic and copies ran while one was open for 0% of the time, Pallas kernels for 44%

profile of v2, /device:TPU:96, one launch (start us, length us, event | category | flops | bytes accessed | tf_op | source)
XLA Modules:
  0.0 50.9 jit_solution(2661453110371953986)
XLA Ops:
  0.0 1.3 %constant_dynamic-slice_fusion = (bf16[8,8,4096]{2,1,0:T(8,128)(2,1)S(1)}, bf16[8,8,4096]{2,1,0:T(8,128)(2,1)S(1)}) fusion(bf16[8,64,4096]{2,1,0:T(8,128)(2,1)} %refs_3_.3, s32[]{:T(128)S(6)} %select_n.7, s32[]{:T(128)S(6)} %select_n.6), kind=kLoop, calls=%fused_computation | loop fusion | bytes 2097160 | tf_op jit(solution)/shard_map/dynamic_slice | solution.py:338
  1.3 4.4 %collective-permute-start = (bf16[8,8,4096]{2,1,0:T(8,128)(2,1)S(1)}, bf16[8,8,4096]{2,1,0:T(8,128)(2,1)S(1)}, u32[]{:S(2)}, u32[]{:S(2)}) collective-permute-start(bf16[8,8,4096]{2,1,0:T(8,128)(2,1)S(1)} %get-tuple-element.10), channel_id=1, source_target_pairs={{1,2},{3,4},{5,6},{7,8},{9,10},{11,12},{13,14},{2,1},{4,3},{6,5},{... | collective-permute-start | bytes 1572872 | tf_op jit(solution)/shard_map/ppermute | solution.py:337
  5.7 0.9 %collective-permute-start.1 = (bf16[8,8,4096]{2,1,0:T(8,128)(2,1)S(1)}, bf16[8,8,4096]{2,1,0:T(8,128)(2,1)S(1)}, u32[]{:S(2)}, u32[]{:S(2)}) collective-permute-start(bf16[8,8,4096]{2,1,0:T(8,128)(2,1)S(1)} %get-tuple-element.9), channel_id=1, source_target_pairs={{0,1},{2,3},{4,5},{6,7},{8,9},{10,11},{12,13},{14,15},{1,0},{3,2},... | collective-permute-start | bytes 1572872 | tf_op jit(solution)/shard_map/ppermute | solution.py:338
  6.6 0.0 copy-start.1
  6.6 0.0 copy-start.2
  6.6 11.5 %embed_inner.1 = (bf16[8,72,512]{2,1,0:T(8,128)(2,1)}, bf16[8192,512]{1,0:T(8,128)(2,1)}) custom-call(f32[1,512]{1,0:T(1,128)} %bitcast.1, bf16[512,512]{1,0:T(8,128)(2,1)} %refs_1_.1, bf16[512,512]{1,0:T(8,128)(2,1)} %refs_2_.1, bf16[8,64,4096]{2,1,0:T(8,128)(2,1)} %refs_3_.3, bf16[8,32,32,512]{3,2,1,0:T(8,128)(2,1)} %refs_4_.3, s32[8,4,256]{2,1,0:T(4,128)} %refs_5_.3, ...), custom_call_target="tpu_custom_call" | custom-call | flops 6442450944 | bytes 13631488 | tf_op jit(solution)/shard_map/embed_inner/pallas_call | solution.py:271
  18.1 4.4 %all-to-all-start = ((bf16[8,72,512]{2,1,0:T(8,128)(2,1)}), bf16[8,72,512]{2,1,0:T(8,128)(2,1)S(1)}, u32[]{:S(2)}, u32[]{:S(2)}) async-start(bf16[8,72,512]{2,1,0:T(8,128)(2,1)} %get-tuple-element.7), calls=%async_computation | async-start | bytes 1179648 | tf_op jit(solution)/shard_map/all_to_all | solution.py:326
  22.5 0.0 collective-permute-done.refs_0_
  22.5 0.0 collective-permute-done.1.refs_1_
  22.5 0.0 copy-done.1
  22.5 0.0 copy-done.2
  22.5 0.0 copy-start
  22.6 10.9 %embed_edge.1 = bf16[8,72,512]{2,1,0:T(8,128)(2,1)S(1)} custom-call(bf16[8,8,4096]{2,1,0:T(8,128)(2,1)S(1)} %collective-permute-done.refs_0_, bf16[8,8,4096]{2,1,0:T(8,128)(2,1)S(1)} %collective-permute-done.1.refs_1_, bf16[8192,512]{1,0:T(8,128)(2,1)} %get-tuple-element.8.refs_2_, bf16[8,64,4096]{2,1,0:T(8,128)(2,1)} %refs_3_.3, ...), custom_call_target="tpu_custom_call" | custom-call | flops 6442450944 | bytes 13631488 | tf_op jit(solution)/shard_map/embed_edge/pallas_call | solution.py:271
  33.5 0.0 all-to-all-done.inner_ref
  33.5 15.9 %all_to_all.10.outer_ref = bf16[8,72,512]{2,1,0:T(8,128)(2,1)S(1)} all-to-all(bf16[8,72,512]{2,1,0:T(8,128)(2,1)S(1)} %embed_edge.1), channel_id=1, replica_groups=mesh['var'=8,'space'=16] {'var'}, dimensions={0} | all-to-all | bytes 1179648 | tf_op jit(solution)/shard_map/all_to_all | solution.py:326
  49.5 0.0 copy-done
  49.5 1.4 %finish.1 = bf16[4,32,512]{2,1,0:T(8,128)(2,1)} custom-call(bf16[8,72,512]{2,1,0:T(8,128)(2,1)S(1)} %all-to-all-done.inner_ref, bf16[8,72,512]{2,1,0:T(8,128)(2,1)S(1)} %all_to_all.10.outer_ref, bf16[512,512]{1,0:T(8,128)(2,1)S(1)} %copy-done), custom_call_target="tpu_custom_call" | custom-call | flops 67108864 | bytes 2097152 | tf_op jit(solution)/shard_map/finish/pallas_call | solution.py:316
Async XLA Ops:
  1.3 21.2 %collective-permute-start = (bf16[8,8,4096]{2,1,0:T(8,128)(2,1)S(1)}, bf16[8,8,4096]{2,1,0:T(8,128)(2,1)S(1)}, u32[]{:S(2)}, u32[]{:S(2)}) collective-permute-start(bf16[8,8,4096]{2,1,0:T(8,128)(2,1)S(1)} %get-tuple-element.10), channel_id=1, source_target_pairs={{1,2},{3,4},{5,6},{7,8},{9,10},{11,12},{13,14},{2,1},{4,3},{6,5},{... | collective-permute-start | bytes 1572872 | tf_op jit(solution)/shard_map/ppermute | solution.py:337
  5.7 16.9 %collective-permute-start.1 = (bf16[8,8,4096]{2,1,0:T(8,128)(2,1)S(1)}, bf16[8,8,4096]{2,1,0:T(8,128)(2,1)S(1)}, u32[]{:S(2)}, u32[]{:S(2)}) collective-permute-start(bf16[8,8,4096]{2,1,0:T(8,128)(2,1)S(1)} %get-tuple-element.9), channel_id=1, source_target_pairs={{0,1},{2,3},{4,5},{6,7},{8,9},{10,11},{12,13},{14,15},{1,0},{3,2},... | collective-permute-start | bytes 1572872 | tf_op jit(solution)/shard_map/ppermute | solution.py:338
  6.6 15.9 %copy-start.1 = (s32[8,4,256]{2,1,0:T(4,128)S(1)}, s32[8,4,256]{2,1,0:T(4,128)}, u32[]{:S(2)}) copy-start(s32[8,4,256]{2,1,0:T(4,128)} %refs_5_.3) | copy-start | bytes 98308
  6.6 16.0 %copy-start.2 = (bf16[8,512]{1,0:T(8,128)(2,1)S(1)}, bf16[8,512]{1,0:T(8,128)(2,1)}, u32[]{:S(2)}) copy-start(bf16[8,512]{1,0:T(8,128)(2,1)} %refs_6_.3) | copy-start | bytes 24580
  18.1 15.4 %all-to-all-start = ((bf16[8,72,512]{2,1,0:T(8,128)(2,1)}), bf16[8,72,512]{2,1,0:T(8,128)(2,1)S(1)}, u32[]{:S(2)}, u32[]{:S(2)}) async-start(bf16[8,72,512]{2,1,0:T(8,128)(2,1)} %get-tuple-element.7), calls=%async_computation | async-start | bytes 1179648 | tf_op jit(solution)/shard_map/all_to_all | solution.py:326
  22.5 26.9 %copy-start = (bf16[512,512]{1,0:T(8,128)(2,1)S(1)}, bf16[512,512]{1,0:T(8,128)(2,1)}, u32[]{:S(2)}) copy-start(bf16[512,512]{1,0:T(8,128)(2,1)} %wo_ref.1) | copy-start | bytes 1572868
